TPU v7x, 256 devices: a whole 4x4x8 slice. The times are simulated.
256 devices in a mesh: seq: 32 (over y, z), head: 8 (over x, core).
Axes of the slice: x: 4, y: 4, z: 8, core: 2. Of those that a mesh axis runs over, the one named last changes fastest.
Arguments:
- queries: bfloat16 [32768, 32, 128], P('seq', 'head'), may hold values from -6 to 6
- key_rows: bfloat16 [32768, 32, 128], P('seq', 'head'), may hold values from -6 to 6
- value_rows: bfloat16 [32768, 32, 128], P('seq', 'head'), may hold values from -6 to 6
- out_grad: bfloat16 [32768, 4096], P('seq', 'head'), may hold values from -6 to 6
- out_weight: bfloat16 [32, 128, 4096], P('head'), may hold values from -0.09375 to 0.09375
Outputs:
- query_grad: bfloat16 [32768, 32, 128], P('seq', 'head')
- key_grad: bfloat16 [32768, 32, 128], P('seq', 'head')
- value_grad: bfloat16 [32768, 32, 128], P('seq', 'head')
All inputs are finite; a program needn't handle non-finite values.
Results may differ from a plain program's by a relative error of at most 0.0058.
Values may be sent and summed in bfloat16 or wider, within the bound.
No kernel may reach another device: no remote copies, remote signals or barrier semaphores. Data moves between devices by JAX's collectives and lax.ppermute only.
A program may use at most 128 MiB of HBM per device.

v0:
```python
import math
import jax
import jax.numpy as jnp
from jax import lax
from jax.sharding import PartitionSpec as P

BLOCK = 256


def body(queries, key_rows, value_rows, out_grad, out_weight):
    tokens = queries.shape[0]
    heads = queries.shape[1]
    depth = queries.shape[2]
    blocks = tokens // BLOCK
    factor = 1.0 / math.sqrt(depth * tokens * lax.axis_size("seq"))
    attn_grad = jnp.einsum(
        "tm,hdm->thd",
        lax.all_gather(out_grad, "head", axis=1, tiled=True),
        out_weight,
        preferred_element_type=jnp.float32,
    ).astype(jnp.bfloat16)
    layout = (blocks, BLOCK, heads, depth)
    query_blocks = queries.reshape(layout)
    key_blocks = key_rows.reshape(layout)
    value_blocks = value_rows.reshape(layout)
    grad_blocks = attn_grad.reshape(layout)
    kv_parts = jnp.einsum(
        "bthd,bthe->bhde", key_blocks, value_blocks, preferred_element_type=jnp.float32
    )
    qg_parts = jnp.einsum(
        "bthd,bthe->bhde", query_blocks, grad_blocks, preferred_element_type=jnp.float32
    )
    kv_total = jnp.sum(kv_parts, 0)
    qg_total = jnp.sum(qg_parts, 0)
    shards = lax.axis_size("seq")
    stacked = jnp.stack([kv_total, qg_total]).reshape(2, shards, -1)
    pieces = lax.all_to_all(stacked, "seq", split_axis=1, concat_axis=1, tiled=True)
    forward_sums = jnp.cumsum(pieces[0], 0) - pieces[0]
    reverse_sums = jnp.cumsum(pieces[1][::-1], 0)[::-1] - pieces[1]
    totals = lax.all_to_all(
        jnp.stack([forward_sums, reverse_sums]), "seq", split_axis=1, concat_axis=1, tiled=True
    )
    totals = totals.reshape(2, heads, depth, depth)
    before = totals[0]
    after = totals[1]
    first_zero = jnp.zeros((1, heads, depth, depth), jnp.float32)
    running = jnp.cumsum(kv_parts, 0)
    prefix = before[None] + jnp.concatenate([first_zero, running[:-1]], 0)
    backward_sums = jnp.cumsum(qg_parts[::-1], 0)[::-1]
    suffix = after[None] + jnp.concatenate([backward_sums[1:], first_zero], 0)
    prefix_bf = prefix.astype(jnp.bfloat16)
    suffix_bf = suffix.astype(jnp.bfloat16)
    causal = jnp.tril(jnp.ones((BLOCK, BLOCK), bool))
    qk_scores = jnp.einsum(
        "bthd,bshd->bhts", query_blocks, key_blocks, preferred_element_type=jnp.float32
    )
    qk_scores = jnp.where(causal, qk_scores, 0.0).astype(jnp.bfloat16)
    grad_scores = jnp.einsum(
        "bthd,bshd->bhts", grad_blocks, value_blocks, preferred_element_type=jnp.float32
    )
    grad_scores = jnp.where(causal, grad_scores, 0.0).astype(jnp.bfloat16)
    query_grad = jnp.einsum(
        "bhts,bshd->bthd", grad_scores, key_blocks, preferred_element_type=jnp.float32
    )
    query_grad = query_grad + jnp.einsum(
        "bthe,bhde->bthd", grad_blocks, prefix_bf, preferred_element_type=jnp.float32
    )
    key_grad = jnp.einsum(
        "bhts,bthd->bshd", grad_scores, query_blocks, preferred_element_type=jnp.float32
    )
    key_grad = key_grad + jnp.einsum(
        "bshe,bhde->bshd", value_blocks, suffix_bf, preferred_element_type=jnp.float32
    )
    value_grad = jnp.einsum(
        "bhts,bthe->bshe", qk_scores, grad_blocks, preferred_element_type=jnp.float32
    )
    value_grad = value_grad + jnp.einsum(
        "bshd,bhde->bshe", key_blocks, suffix_bf, preferred_element_type=jnp.float32
    )
    final_shape = (tokens, heads, depth)
    return (
        (factor * query_grad).astype(jnp.bfloat16).reshape(final_shape),
        (factor * key_grad).astype(jnp.bfloat16).reshape(final_shape),
        (factor * value_grad).astype(jnp.bfloat16).reshape(final_shape),
    )


def solution(mesh):
    placed = (
        P("seq", "head", None),
        P("seq", "head", None),
        P("seq", "head", None),
        P("seq", "head"),
        P("head", None, None),
    )
    return jax.shard_map(
        body,
        mesh=mesh,
        in_specs=placed,
        out_specs=(P("seq", "head", None), P("seq", "head", None), P("seq", "head", None)),
        check_vma=False,
    )
```

profile of v0, /device:TPU:32, one launch (start us, length us, event | category | flops | bytes accessed | tf_op | source)
XLA Modules:
  0.0 155.0 jit_solution(7390798430991049583)
XLA Ops:
  7.9 2.1 %fusion.38 = (f32[4,128,128]{2,1,0:T(8,128)S(1)}, f32[4,4,128,128]{3,2,1,0:T(8,128)S(1)}) fusion(bf16[4,256,4,128]{3,2,1,0:T(4,128)(2,1)} %bitcast.53, bf16[4,256,4,128]{3,2,1,0:T(4,128)(2,1)} %bitcast.46), kind=kOutput, calls=%fused_computation.48 | convolution fusion | flops 134414336 | bytes 3407872 | tf_op jit(solution)/shard_map/bthd,bthe->bhde/dot_general | solution.py:27
  10.0 54.7 %all-gather.2.cloned.1.call-done = bf16[1024,4096]{1,0:T(8,128)(2,1)} async-done(((bf16[1024,512]{1,0:T(8,128)(2,1)}), bf16[1024,4096]{1,0:T(8,128)(2,1)}) %all-gather.2.cloned.1.call-update) | async-done | bytes 8388624 | tf_op jit(solution)/shard_map/all_gather | solution.py:18
  64.7 8.2 %fusion.7 = bf16[1024,4,128]{2,0,1:T(8,128)(2,1)S(1)} fusion(bf16[4,128,4096]{2,1,0:T(8,128)(2,1)} %param.9, bf16[1024,4096]{1,0:T(8,128)(2,1)} %all-gather.2.cloned.1.call-done), kind=kOutput, calls=%fused_computation.12 | convolution fusion | flops 4295491584 | bytes 13631488 | tf_op jit(solution)/shard_map/tm,hdm->thd/dot_general | solution.py:16
  73.0 1.2 fusion.37
  74.2 1.1 copy.83
  75.4 1.2 copy.84
  76.6 10.1 %all-to-all-start = ((f32[2,32,2048]{2,0,1:T(2,128)}), f32[2,32,2048]{2,0,1:T(2,128)}, u32[]{:S(2)}, u32[]{:S(2)}) async-start(f32[2,32,2048]{2,0,1:T(2,128)} %copy.84), calls=%async_computation | async-start | bytes 1048576 | tf_op jit(solution)/shard_map/all_to_all | solution.py:37
  87.6 1.0 copy-done.9
  89.5 0.9 slice.31
  90.9 1.9 %select_convert_fusion.1 = bf16[4,4,256,256]{3,2,1,0:T(8,128)(2,1)S(1)} fusion(pred[256,256]{1,0:T(8,128)(4,1)S(1)} %iota_compare_fusion, bf16[4,256,4,128]{3,2,1,0:T(4,128)(2,1)S(1)} %bitcast.54, bf16[4,256,4,128]{3,1,0,2:T(8,128)(2,1)} %bitcast.57), kind=kOutput, calls=%fused_computation.3 | convolution fusion | flops 270532608 | bytes 4259840 | tf_op jit(solution)/shard_map/bthd,bshd->bhts/dot_general | solution.py:58
  92.9 12.0 %all-to-all-done = f32[2,32,2048]{2,0,1:T(2,128)} async-done(((f32[2,32,2048]{2,0,1:T(2,128)}), f32[2,32,2048]{2,0,1:T(2,128)}, u32[]{:S(2)}, u32[]{:S(2)}) %all-to-all-start) | async-done | bytes 524320 | tf_op jit(solution)/shard_map/all_to_all | solution.py:37
  104.9 1.7 %fusion.36 = (f32[1,32,2048]{2,0,1:T(1,128)S(1)}, f32[1,32,2048]{2,0,1:T(1,128)S(1)}) fusion(f32[2,32,2048]{2,0,1:T(2,128)} %all-to-all-done), kind=kLoop, calls=%fused_computation.46 | loop fusion | bytes 1048576 | tf_op jit(solution)/shard_map/slice | solution.py:38
  108.1 1.2 copy.87
  109.3 4.9 %all-to-all-start.1 = ((f32[2,32,2048]{2,0,1:T(2,128)}), f32[2,32,2048]{2,0,1:T(2,128)}, u32[]{:S(2)}, u32[]{:S(2)}) async-start(f32[2,32,2048]{2,0,1:T(2,128)} %copy.87), calls=%async_computation.1 | async-start | bytes 1048576 | tf_op jit(solution)/shard_map/all_to_all | solution.py:40
  114.2 3.4 %fusion.13 = f32[4,4,256,128]{3,2,1,0:T(8,128)} fusion(bf16[4,4,256,256]{3,2,1,0:T(8,128)(2,1)S(1)} %select_convert_fusion.1, bf16[4,256,4,128]{3,2,1,0:T(4,128)(2,1)} %bitcast.50), kind=kOutput, calls=%fused_computation.18 | convolution fusion | flops 268435456 | bytes 5242880 | tf_op jit(solution)/shard_map/bhts,bthd->bshd/dot_general | solution.py:68
  117.6 2.0 %fusion.24 = f32[4,4,256,128]{3,2,1,0:T(8,128)} fusion(bf16[4,4,256,256]{3,2,1,0:T(8,128)(2,1)S(1)} %select_convert_fusion.1, bf16[4,256,4,128]{3,2,1,0:T(4,128)(2,1)S(1)} %bitcast.47), kind=kOutput, calls=%fused_computation.28 | convolution fusion | flops 268435456 | bytes 5242880 | tf_op jit(solution)/shard_map/bhts,bshd->bthd/dot_general | solution.py:62
  119.7 3.9 %fusion.6 = f32[4,4,128,256]{3,2,1,0:T(8,128)} fusion(pred[256,256]{1,0:T(8,128)(4,1)S(1)} %iota_compare_fusion, bf16[4,256,4,128]{3,2,1,0:T(4,128)(2,1)} %bitcast.51, bf16[4,256,4,128]{3,2,1,0:T(4,128)(2,1)S(1)} %bitcast.48, bf16[4,256,4,128]{3,1,0,2:T(8,128)(2,1)} %bitcast.58), kind=kOutput, calls=%fused_computation.11 | convolution fusion | flops 538968064 | bytes 5308416 | tf_op jit(solution)/shard_map/bhts,bthe->bshe/dot_general | solution.py:74
  123.6 8.1 %all-to-all-done.1 = f32[2,32,2048]{2,0,1:T(2,128)} async-done(((f32[2,32,2048]{2,0,1:T(2,128)}), f32[2,32,2048]{2,0,1:T(2,128)}, u32[]{:S(2)}, u32[]{:S(2)}) %all-to-all-start.1) | async-done | bytes 524320 | tf_op jit(solution)/shard_map/all_to_all | solution.py:40
  131.7 2.5 %fusion.35 = (f32[1,32,2048]{2,0,1:T(1,128)S(1)}, f32[1,32,2048]{2,0,1:T(1,128)}) fusion(f32[2,32,2048]{2,0,1:T(2,128)} %all-to-all-done.1), kind=kLoop, calls=%fused_computation.45 | loop fusion | bytes 1048576 | tf_op jit(solution)/shard_map/slice | solution.py:45
  134.3 3.0 %fusion.10 = bf16[4,256,4,128]{1,3,2,0:T(8,128)(2,1)} fusion(f32[4,4,128,256]{3,2,1,0:T(8,128)} %fusion.6, bf16[4,256,4,128]{3,2,1,0:T(4,128)(2,1)S(1)} %bitcast.49, f32[3,4,128,128]{2,3,1,0:T(8,128)S(1)} %copy-done.3, f32[4,128,128]{1,2,0:T(8,128)S(1)} %copy.93), kind=kOutput, calls=%fused_computation.13 | convolution fusion | flops 136314880 | bytes 5242880 | tf_op jit(solution)/shard_map/bshd,bhde->bshe/dot_general | solution.py:77
  137.3 2.4 %copy.102 = bf16[4,256,4,128]{3,1,0,2:T(8,128)(2,1)} copy(bf16[4,256,4,128]{1,3,2,0:T(8,128)(2,1)} %fusion.10) | data formatting | bytes 2097152 | tf_op jit(solution)/shard_map/convert_element_type | solution.py:84
  139.7 3.1 %copy.105 = bf16[1024,4,128]{2,1,0:T(4,128)(2,1)} copy(bf16[1024,4,128]{2,0,1:T(8,128)(2,1)} %bitcast.60) | data formatting | bytes 2097152
  143.5 1.8 %copy.104 = bf16[1024,4,128]{2,1,0:T(4,128)(2,1)} copy(bf16[1024,4,128]{2,0,1:T(8,128)(2,1)S(1)} %bitcast.61) | data formatting | bytes 2097152
  146.4 1.8 %copy.103 = bf16[1024,4,128]{2,1,0:T(4,128)(2,1)} copy(bf16[1024,4,128]{2,0,1:T(8,128)(2,1)S(1)} %bitcast.62) | data formatting | bytes 2097152
  (47 shorter events, 6.4 us)
Async XLA Ops:
  7.2 57.6 %all-gather.2.cloned.1.call-start = ((), (), s32[]{:S(2)}) async-start(), calls=%async_computation.2 | async-start | bytes 9437184 | tf_op jit(solution)/shard_map/all_gather | solution.py:18
  10.0 62.9 %copy-start.4 = (bf16[1024,4,128]{2,1,0:T(4,128)(2,1)S(1)}, bf16[1024,4,128]{2,1,0:T(4,128)(2,1)}, u32[]{:S(2)}) copy-start(bf16[1024,4,128]{2,1,0:T(4,128)(2,1)} %param.5) | copy-start | bytes 3145732
  72.9 1.3 copy-start.7
  76.6 28.3 %all-to-all-start = ((f32[2,32,2048]{2,0,1:T(2,128)}), f32[2,32,2048]{2,0,1:T(2,128)}, u32[]{:S(2)}, u32[]{:S(2)}) async-start(f32[2,32,2048]{2,0,1:T(2,128)} %copy.84), calls=%async_computation | async-start | bytes 1048576 | tf_op jit(solution)/shard_map/all_to_all | solution.py:37
  87.5 1.0 copy-start.9
  89.4 1.5 copy-start.5
  109.3 22.4 %all-to-all-start.1 = ((f32[2,32,2048]{2,0,1:T(2,128)}), f32[2,32,2048]{2,0,1:T(2,128)}, u32[]{:S(2)}, u32[]{:S(2)}) async-start(f32[2,32,2048]{2,0,1:T(2,128)} %copy.87), calls=%async_computation.1 | async-start | bytes 1048576 | tf_op jit(solution)/shard_map/all_to_all | solution.py:40
  114.2 3.4 %copy-start = (bf16[1024,4,128]{2,1,0:T(4,128)(2,1)S(1)}, bf16[1024,4,128]{2,1,0:T(4,128)(2,1)}, u32[]{:S(2)}) copy-start(bf16[1024,4,128]{2,1,0:T(4,128)(2,1)} %param.6) | copy-start | bytes 3145732
  123.6 10.7 %copy-start.3 = (f32[3,4,128,128]{2,3,1,0:T(8,128)S(1)}, f32[3,4,128,128]{2,3,1,0:T(8,128)}, u32[]{:S(2)}) copy-start(f32[3,4,128,128]{2,3,1,0:T(8,128)} %slice.31) | copy-start | bytes 2359300
  137.3 5.5 %copy-start.2 = (f32[4,4,256,128]{3,2,1,0:T(8,128)S(1)}, f32[4,4,256,128]{3,2,1,0:T(8,128)}, u32[]{:S(2)}) copy-start(f32[4,4,256,128]{3,2,1,0:T(8,128)} %fusion.13) | copy-start | bytes 6291460
  139.7 3.1 %copy-start.6 = (bf16[1024,4,128]{2,1,0:T(4,128)(2,1)S(1)}, bf16[1024,4,128]{2,1,0:T(4,128)(2,1)}, u32[]{:S(2)}) copy-start(bf16[1024,4,128]{2,1,0:T(4,128)(2,1)} %param.7) | copy-start | bytes 3145732
  143.3 1.9 %copy-start.1 = (f32[4,4,256,128]{3,2,1,0:T(8,128)S(1)}, f32[4,4,256,128]{3,2,1,0:T(8,128)}, u32[]{:S(2)}) copy-start(f32[4,4,256,128]{3,2,1,0:T(8,128)} %fusion.24) | copy-start | bytes 6291460
  143.3 1.9 %copy-start.8 = (bf16[1024,4,128]{2,0,1:T(8,128)(2,1)S(1)}, bf16[1024,4,128]{2,0,1:T(8,128)(2,1)}, u32[]{:S(2)}) copy-start(bf16[1024,4,128]{2,0,1:T(8,128)(2,1)} %copy-done.7) | copy-start | bytes 3145732
  143.3 2.4 %slice-start = ((f32[4,4,128,128]{3,2,1,0:T(8,128)}), f32[3,4,128,128]{3,2,1,0:T(8,128)S(1)}, s32[]{:S(2)}) async-start(f32[4,4,128,128]{3,2,1,0:T(8,128)} %copy-done.9), calls=%async_computation.3 | async-start | bytes 1572864 | tf_op jit(solution)/shard_map/slice | solution.py:48
  143.4 2.5 %copy-start.10 = (f32[1,32,2048]{2,0,1:T(1,128)S(1)}, f32[1,32,2048]{2,0,1:T(1,128)}, u32[]{:S(2)}) copy-start(f32[1,32,2048]{2,0,1:T(1,128)} %get-tuple-element.13) | copy-start | bytes 786436
Sparse Core Ops, SparseCore 0:
  9.8 54.8 all-gather.1
where the time goes:
time: 156 us; the launch traced here: 155 us
  waiting for transfers between devices  75.5 us (48%)
  matrix products  26.8 us (17%)
  local copies, waits for them, and re-layouts  21.1 us (14%)
  starting transfers between devices  15.1 us (10%)
  between operations  14.3 us (9%)
  other arithmetic  2.3 us (1%)
    all_gather x1, waiting for transfers between devices, body(): lax.all_gather(out_grad, 'head', axis=1, tiled=True)  54.7 us
    all_to_all x1, waiting for transfers between devices, body(): lax.all_to_all(stacked, 'seq', split_axis=1, concat_axis=1, tiled=True)  12 us
    all_to_all x1, starting transfers between devices, body(): lax.all_to_all(stacked, 'seq', split_axis=1, concat_axis=1, tiled=True)  10.1 us
    unnamed x27, local copies, waits for them, and re-layouts  8.39 us
    dot_general x1, matrix products, body(): jnp.einsum('tm,hdm->thd', lax.all_gather(out_grad, 'head', axis=1, tiled=...  8.22 us
    all_to_all x1, waiting for transfers between devices, body(): lax.all_to_all(jnp.stack([forward_sums, reverse_sums]), 'seq', split_axis...  8.12 us
    all_to_all x1, starting transfers between devices, body(): lax.all_to_all(jnp.stack([forward_sums, reverse_sums]), 'seq', split_axis...  4.9 us
    dot_general x1, matrix products, body(): jnp.einsum('bhts,bthe->bshe', qk_scores, grad_blocks, preferred_element_t...  3.89 us
  transfers between devices with their start and end apart: 3, of which 3 were waited for; matrix products, arithmetic and copies ran while one was open for 10% of the time, Pallas kernels for 0%

commit v1 on v0

--- a/solution.py
+++ b/solution.py
@@ -7,17 +7,38 @@
 BLOCK = 256
 
 
+def product_in_turn(x, axis, dim, term):
+    devices, index, width = (lax.axis_size(axis), lax.axis_index(axis), x.shape[dim])
+    right = [(i, (i + 1) % devices) for i in range(devices)]
+    backward = [(i, (i - 1) % devices) for i in range(devices)]
+    halfway = devices // 2
+    from_left = from_right = x
+    total = term(x, index * width)
+    for turn in range(1, halfway + 1):
+        from_left = lax.ppermute(from_left, axis, right)
+        if turn < devices - halfway:
+            from_right = lax.ppermute(from_right, axis, backward)
+            total = total + term(from_right, (index + turn) % devices * width)
+        total = total + term(from_left, (index - turn) % devices * width)
+    return total
+
+
 def body(queries, key_rows, value_rows, out_grad, out_weight):
     tokens = queries.shape[0]
     heads = queries.shape[1]
     depth = queries.shape[2]
     blocks = tokens // BLOCK
     factor = 1.0 / math.sqrt(depth * tokens * lax.axis_size("seq"))
-    attn_grad = jnp.einsum(
-        "tm,hdm->thd",
-        lax.all_gather(out_grad, "head", axis=1, tiled=True),
-        out_weight,
-        preferred_element_type=jnp.float32,
+    attn_grad = product_in_turn(
+        out_grad,
+        "head",
+        1,
+        lambda own_block, offset: jnp.einsum(
+            "tm,hdm->thd",
+            own_block,
+            lax.dynamic_slice_in_dim(out_weight, offset, own_block.shape[1], axis=2),
+            preferred_element_type=jnp.float32,
+        ),
     ).astype(jnp.bfloat16)
     layout = (blocks, BLOCK, heads, depth)
     query_blocks = queries.reshape(layout)

time: 156 us -> 138 us (0.88)
  the two profiles are of different devices: /device:TPU:32 before, /device:TPU:38 now
where the time goes in v1:
time: 138 us; the launch traced here: 137 us
  waiting for transfers between devices  53.6 us (39%)
  matrix products  32.8 us (24%)
  local copies, waits for them, and re-layouts  23.7 us (17%)
  starting transfers between devices  22.5 us (16%)
  other arithmetic  3.33 us (2%)
    ppermute x4, waiting for transfers between devices, product_in_turn(): from_left = lax.ppermute(from_left, axis, right)  35.2 us
    dot_general x8, matrix products, body(): jnp.einsum('tm,hdm->thd', own_block, lax.dynamic_slice_in_dim(out_weight,...  12.6 us
    all_to_all x1, starting transfers between devices, body(): lax.all_to_all(stacked, 'seq', split_axis=1, concat_axis=1, tiled=True)  11.4 us
    all_to_all x1, waiting for transfers between devices, body(): lax.all_to_all(jnp.stack([forward_sums, reverse_sums]), 'seq', split_axis...  8.28 us
    all_to_all x1, waiting for transfers between devices, body(): lax.all_to_all(stacked, 'seq', split_axis=1, concat_axis=1, tiled=True)  8.18 us
    unnamed x31, local copies, waits for them, and re-layouts  7.87 us
    all_to_all x1, starting transfers between devices, body(): lax.all_to_all(jnp.stack([forward_sums, reverse_sums]), 'seq', split_axis...  5.36 us
    ppermute x3, starting transfers between devices, product_in_turn(): from_right = lax.ppermute(from_right, axis, backward)  5.32 us
  transfers between devices with their start and end apart: 9, of which 7 were waited for; matrix products, arithmetic and copies ran while one was open for 24% of the time, Pallas kernels for 0%

profile of v1, /device:TPU:38, one launch (start us, length us, event | category | flops | bytes accessed | tf_op | source)
XLA Modules:
  0.0 137.0 jit_solution(13262865409520311876)
XLA Ops:
  2.4 12.7 %collective-permute-done.1 = bf16[1024,512]{1,0:T(8,128)(2,1)S(1)} collective-permute-done((bf16[1024,512]{1,0:T(8,128)(2,1)}, bf16[1024,512]{1,0:T(8,128)(2,1)S(1)}, u32[]{:S(2)}, u32[]{:S(2)}) %collective-permute-start.1) | collective-permute-done | bytes 1048608 | tf_op jit(solution)/shard_map/ppermute | solution.py:18
  15.1 1.8 %collective-permute-start.2 = (bf16[1024,512]{1,0:T(8,128)(2,1)}, bf16[1024,512]{1,0:T(8,128)(2,1)}, u32[]{:S(2)}, u32[]{:S(2)}) collective-permute-start(bf16[1024,512]{1,0:T(8,128)(2,1)} %collective-permute-done), channel_id=1, source_target_pairs={{0,7},{1,0},{2,1},{3,2},{4,3},{5,4},{6,5},{7,6},{8,15},{9,8},{10,9... | collective-permute-start | bytes 3145736 | tf_op jit(solution)/shard_map/ppermute | solution.py:20
  16.9 12.4 %collective-permute-done.3 = bf16[1024,512]{1,0:T(8,128)(2,1)S(1)} collective-permute-done((bf16[1024,512]{1,0:T(8,128)(2,1)S(1)}, bf16[1024,512]{1,0:T(8,128)(2,1)S(1)}, u32[]{:S(2)}, u32[]{:S(2)}) %collective-permute-start.3) | collective-permute-done | bytes 1048608 | tf_op jit(solution)/shard_map/ppermute | solution.py:18
  29.3 2.1 %fusion.64 = (f32[4,128,128]{2,1,0:T(8,128)S(1)}, f32[4,4,128,128]{3,2,1,0:T(8,128)S(1)}) fusion(bf16[4,256,4,128]{3,2,1,0:T(4,128)(2,1)} %bitcast.86, bf16[4,256,4,128]{3,2,1,0:T(4,128)(2,1)} %bitcast.76), kind=kOutput, calls=%fused_computation.77 | convolution fusion | flops 134414336 | bytes 3407872 | tf_op jit(solution)/shard_map/bthd,bthe->bhde/dot_general | solution.py:48
  32.3 1.9 %fusion.21 = f32[4,128,1024]{2,1,0:T(8,128)S(1)} fusion(bf16[1024,512]{1,0:T(8,128)(2,1)S(1)} %copy-done.11, bf16[4,128,4096]{2,1,0:T(8,128)(2,1)} %param.9, s32[]{:T(128)S(6)} %select_n.64), kind=kOutput, calls=%fused_computation.28 | convolution fusion | flops 536870912 | bytes 3670020 | tf_op jit(solution)/shard_map/tm,hdm->thd/dot_general | solution.py:36
  34.2 2.1 %fusion.17 = f32[4,128,1024]{2,1,0:T(8,128)S(1)} fusion(bf16[1024,512]{1,0:T(8,128)(2,1)} %copy-done.12, bf16[4,128,4096]{2,1,0:T(8,128)(2,1)} %param.9, s32[]{:T(128)S(6)} %select_n.68), kind=kOutput, calls=%fused_computation.24 | convolution fusion | flops 536870912 | bytes 3670020 | tf_op jit(solution)/shard_map/tm,hdm->thd/dot_general | solution.py:36
  38.1 2.0 %fusion.19 = f32[4,128,1024]{2,1,0:T(8,128)S(1)} fusion(bf16[1024,512]{1,0:T(8,128)(2,1)} %collective-permute-done, bf16[4,128,4096]{2,1,0:T(8,128)(2,1)S(1)} %copy-done.8, s32[]{:T(128)S(6)} %select_n.66), kind=kOutput, calls=%fused_computation.26 | convolution fusion | flops 536870912 | bytes 3670020 | tf_op jit(solution)/shard_map/tm,hdm->thd/dot_general | solution.py:36
  40.1 3.5 %collective-permute-done.5 = bf16[1024,512]{1,0:T(8,128)(2,1)} collective-permute-done((bf16[1024,512]{1,0:T(8,128)(2,1)S(1)}, bf16[1024,512]{1,0:T(8,128)(2,1)}, u32[]{:S(2)}, u32[]{:S(2)}) %collective-permute-start.5) | collective-permute-done | bytes 1048608 | tf_op jit(solution)/shard_map/ppermute | solution.py:18
  44.8 2.0 %fusion.15 = f32[4,128,1024]{2,1,0:T(8,128)S(1)} fusion(bf16[1024,512]{1,0:T(8,128)(2,1)} %collective-permute-done.2, bf16[4,128,4096]{2,1,0:T(8,128)(2,1)S(1)} %copy-done.8, s32[]{:T(128)S(6)} %select_n.70), kind=kOutput, calls=%fused_computation.22 | convolution fusion | flops 536870912 | bytes 3670020 | tf_op jit(solution)/shard_map/tm,hdm->thd/dot_general | solution.py:36
  46.8 2.0 %fusion.9 = f32[4,128,1024]{2,1,0:T(8,128)S(1)} fusion(bf16[1024,512]{1,0:T(8,128)(2,1)} %collective-permute-done.5, bf16[4,128,4096]{2,1,0:T(8,128)(2,1)S(1)} %copy-done.8, s32[]{:T(128)S(6)} %select_n.76), kind=kOutput, calls=%fused_computation.16 | convolution fusion | flops 536870912 | bytes 3670020 | tf_op jit(solution)/shard_map/tm,hdm->thd/dot_general | solution.py:36
  48.8 2.0 %collective-permute-done.4 = bf16[1024,512]{1,0:T(8,128)(2,1)S(1)} collective-permute-done((bf16[1024,512]{1,0:T(8,128)(2,1)}, bf16[1024,512]{1,0:T(8,128)(2,1)S(1)}, u32[]{:S(2)}, u32[]{:S(2)}) %collective-permute-start.4) | collective-permute-done | bytes 1048608 | tf_op jit(solution)/shard_map/ppermute | solution.py:20
  51.5 6.6 %collective-permute-done.6 = bf16[1024,512]{1,0:T(8,128)(2,1)S(1)} collective-permute-done((bf16[1024,512]{1,0:T(8,128)(2,1)}, bf16[1024,512]{1,0:T(8,128)(2,1)S(1)}, u32[]{:S(2)}, u32[]{:S(2)}) %collective-permute-start.6) | collective-permute-done | bytes 1048608 | tf_op jit(solution)/shard_map/ppermute | solution.py:18
  64.5 11.4 %all-to-all-start = ((f32[2,32,2048]{2,0,1:T(2,128)}), f32[2,32,2048]{2,0,1:T(2,128)}, u32[]{:S(2)}, u32[]{:S(2)}) async-start(f32[2,32,2048]{2,0,1:T(2,128)} %copy.84), calls=%async_computation | async-start | bytes 1048576 | tf_op jit(solution)/shard_map/all_to_all | solution.py:58
  80.2 2.4 %copy.76 = bf16[4,256,4,128]{3,1,2,0:T(8,128)(2,1)} copy(bf16[4,256,4,128]{1,0,3,2:T(4,128)(2,1)} %reshape.40) | data formatting | bytes 2097152 | tf_op jit(solution)/shard_map/reshape | solution.py:47
  82.6 3.2 %select_convert_fusion.1 = bf16[4,4,256,256]{3,2,1,0:T(8,128)(2,1)} fusion(bf16[4,256,4,128]{3,1,2,0:T(8,128)(2,1)} %copy.76, pred[256,256]{1,0:T(8,128)(4,1)S(1)} %iota_compare_fusion, bf16[4,256,4,128]{3,2,1,0:T(4,128)(2,1)S(1)} %bitcast.87), kind=kOutput, calls=%fused_computation.1 | convolution fusion | flops 270532608 | bytes 4259840 | tf_op jit(solution)/shard_map/bthd,bshd->bhts/dot_general | solution.py:79
  85.9 8.2 %all-to-all-done = f32[2,32,2048]{2,0,1:T(2,128)} async-done(((f32[2,32,2048]{2,0,1:T(2,128)}), f32[2,32,2048]{2,0,1:T(2,128)}, u32[]{:S(2)}, u32[]{:S(2)}) %all-to-all-start) | async-done | bytes 524320 | tf_op jit(solution)/shard_map/all_to_all | solution.py:58
  98.5 5.4 %all-to-all-start.1 = ((f32[2,32,2048]{2,0,1:T(2,128)}), f32[2,32,2048]{2,0,1:T(2,128)S(1)}, u32[]{:S(2)}, u32[]{:S(2)}) async-start(f32[2,32,2048]{2,0,1:T(2,128)} %copy.87), calls=%async_computation.1 | async-start | bytes 1048576 | tf_op jit(solution)/shard_map/all_to_all | solution.py:61
  103.9 4.1 %fusion.27 = f32[4,4,256,128]{3,2,1,0:T(8,128)} fusion(bf16[4,4,256,256]{3,2,1,0:T(8,128)(2,1)} %select_convert_fusion.1, bf16[4,256,4,128]{3,2,1,0:T(4,128)(2,1)} %bitcast.83), kind=kOutput, calls=%fused_computation.35 | convolution fusion | flops 268435456 | bytes 5242880 | tf_op jit(solution)/shard_map/bhts,bthd->bshd/dot_general | solution.py:89
  108.0 2.0 %fusion.38 = f32[4,4,256,128]{3,2,1,0:T(8,128)} fusion(bf16[4,4,256,256]{3,2,1,0:T(8,128)(2,1)S(1)} %copy-done.1, bf16[4,256,4,128]{3,2,1,0:T(4,128)(2,1)S(1)} %bitcast.77), kind=kOutput, calls=%fused_computation.45 | convolution fusion | flops 268435456 | bytes 5242880 | tf_op jit(solution)/shard_map/bhts,bshd->bthd/dot_general | solution.py:83
  110.0 3.6 %fusion.4 = f32[4,4,128,256]{3,2,1,0:T(8,128)} fusion(pred[256,256]{1,0:T(8,128)(4,1)S(1)} %iota_compare_fusion, bf16[4,16,4,8,256]{4,3,2,1,0:T(8,128)(2,1)S(1)} %bitcast.82, bf16[4,256,4,128]{3,2,1,0:T(4,128)(2,1)} %bitcast.84, bf16[4,256,4,128]{3,2,1,0:T(4,128)(2,1)S(1)} %bitcast.78), kind=kOutput, calls=%fused_computation.10 | convolution fusion | flops 538968064 | bytes 5308416 | tf_op jit(solution)/shard_map/bhts,bthe->bshe/dot_general | solution.py:95
  113.6 8.3 %all-to-all-done.1 = f32[2,32,2048]{2,0,1:T(2,128)S(1)} async-done(((f32[2,32,2048]{2,0,1:T(2,128)}), f32[2,32,2048]{2,0,1:T(2,128)S(1)}, u32[]{:S(2)}, u32[]{:S(2)}) %all-to-all-start.1) | async-done | bytes 524320 | tf_op jit(solution)/shard_map/all_to_all | solution.py:61
  123.1 3.0 %fusion.5 = bf16[4,256,4,128]{1,3,2,0:T(8,128)(2,1)} fusion(f32[4,4,128,256]{3,2,1,0:T(8,128)} %fusion.4, bf16[4,256,4,128]{3,2,1,0:T(4,128)(2,1)S(1)} %bitcast.79, f32[3,4,128,128]{2,3,1,0:T(8,128)S(1)} %slice.31, f32[4,128,128]{1,2,0:T(8,128)S(1)} %copy.93), kind=kOutput, calls=%fused_computation.11 | convolution fusion | flops 136314880 | bytes 5242880 | tf_op jit(solution)/shard_map/bshd,bhde->bshe/dot_general | solution.py:98
  126.1 2.4 %copy.102 = bf16[4,256,4,128]{3,1,0,2:T(8,128)(2,1)} copy(bf16[4,256,4,128]{1,3,2,0:T(8,128)(2,1)} %fusion.5) | data formatting | bytes 2097152 | tf_op jit(solution)/shard_map/convert_element_type | solution.py:105
  128.6 3.1 %copy.105 = bf16[1024,4,128]{2,1,0:T(4,128)(2,1)} copy(bf16[1024,4,128]{2,0,1:T(8,128)(2,1)} %bitcast.89) | data formatting | bytes 2097152
  (71 shorter events, 27.7 us)
Async XLA Ops:
  0.6 31.7 %copy-start.11 = (bf16[1024,512]{1,0:T(8,128)(2,1)S(1)}, bf16[1024,512]{1,0:T(8,128)(2,1)}, u32[]{:S(2)}) copy-start(bf16[1024,512]{1,0:T(8,128)(2,1)} %param.8) | copy-start | bytes 3145732
  0.6 14.4 %collective-permute-start.1 = (bf16[1024,512]{1,0:T(8,128)(2,1)}, bf16[1024,512]{1,0:T(8,128)(2,1)S(1)}, u32[]{:S(2)}, u32[]{:S(2)}) collective-permute-start(bf16[1024,512]{1,0:T(8,128)(2,1)} %param.8), channel_id=1, source_target_pairs={{0,1},{1,2},{2,3},{3,4},{4,5},{5,6},{6,7},{7,0},{8,9},{9,10},{10,1... | collective-permute-start | bytes 3145736 | tf_op jit(solution)/shard_map/ppermute | solution.py:18
  0.7 14.4 %collective-permute-start = (bf16[1024,512]{1,0:T(8,128)(2,1)}, bf16[1024,512]{1,0:T(8,128)(2,1)}, u32[]{:S(2)}, u32[]{:S(2)}) collective-permute-start(bf16[1024,512]{1,0:T(8,128)(2,1)} %param.8), channel_id=1, source_target_pairs={{0,7},{1,0},{2,1},{3,2},{4,3},{5,4},{6,5},{7,6},{8,15},{9,8},{10,9... | collective-permute-start | bytes 3145736 | tf_op jit(solution)/shard_map/ppermute | solution.py:20
  15.1 14.2 %copy-start.12 = (bf16[1024,512]{1,0:T(8,128)(2,1)}, bf16[1024,512]{1,0:T(8,128)(2,1)S(1)}, u32[]{:S(2)}) copy-start(bf16[1024,512]{1,0:T(8,128)(2,1)S(1)} %collective-permute-done.1) | copy-start | bytes 3145732
  15.1 14.2 %collective-permute-start.3 = (bf16[1024,512]{1,0:T(8,128)(2,1)S(1)}, bf16[1024,512]{1,0:T(8,128)(2,1)S(1)}, u32[]{:S(2)}, u32[]{:S(2)}) collective-permute-start(bf16[1024,512]{1,0:T(8,128)(2,1)S(1)} %collective-permute-done.1), channel_id=1, source_target_pairs={{0,1},{1,2},{2,3},{3,4},{4,5},{5,6},{6,7},{7,0},{8,9},{9,10},{10,1... | collective-permute-start | bytes 3145736 | tf_op jit(solution)/shard_map/ppermute | solution.py:18
  15.1 21.3 %collective-permute-start.2 = (bf16[1024,512]{1,0:T(8,128)(2,1)}, bf16[1024,512]{1,0:T(8,128)(2,1)}, u32[]{:S(2)}, u32[]{:S(2)}) collective-permute-start(bf16[1024,512]{1,0:T(8,128)(2,1)} %collective-permute-done), channel_id=1, source_target_pairs={{0,7},{1,0},{2,1},{3,2},{4,3},{5,4},{6,5},{7,6},{8,15},{9,8},{10,9... | collective-permute-start | bytes 3145736 | tf_op jit(solution)/shard_map/ppermute | solution.py:20
  29.3 14.3 %collective-permute-start.5 = (bf16[1024,512]{1,0:T(8,128)(2,1)S(1)}, bf16[1024,512]{1,0:T(8,128)(2,1)}, u32[]{:S(2)}, u32[]{:S(2)}) collective-permute-start(bf16[1024,512]{1,0:T(8,128)(2,1)S(1)} %collective-permute-done.3), channel_id=1, source_target_pairs={{0,1},{1,2},{2,3},{3,4},{4,5},{5,6},{6,7},{7,0},{8,9},{9,10},{10,1... | collective-permute-start | bytes 3145736 | tf_op jit(solution)/shard_map/ppermute | solution.py:18
  32.3 5.8 %copy-start.8 = (bf16[4,128,4096]{2,1,0:T(8,128)(2,1)S(1)}, bf16[4,128,4096]{2,1,0:T(8,128)(2,1)}, u32[]{:S(2)}) copy-start(bf16[4,128,4096]{2,1,0:T(8,128)(2,1)} %param.9) | copy-start | bytes 12582916
  36.4 14.4 %collective-permute-start.4 = (bf16[1024,512]{1,0:T(8,128)(2,1)}, bf16[1024,512]{1,0:T(8,128)(2,1)S(1)}, u32[]{:S(2)}, u32[]{:S(2)}) collective-permute-start(bf16[1024,512]{1,0:T(8,128)(2,1)} %collective-permute-done.2), channel_id=1, source_target_pairs={{0,7},{1,0},{2,1},{3,2},{4,3},{5,4},{6,5},{7,6},{8,15},{9,8},{10,9... | collective-permute-start | bytes 3145736 | tf_op jit(solution)/shard_map/ppermute | solution.py:20
  43.6 14.4 %collective-permute-start.6 = (bf16[1024,512]{1,0:T(8,128)(2,1)}, bf16[1024,512]{1,0:T(8,128)(2,1)S(1)}, u32[]{:S(2)}, u32[]{:S(2)}) collective-permute-start(bf16[1024,512]{1,0:T(8,128)(2,1)} %collective-permute-done.5), channel_id=1, source_target_pairs={{0,1},{1,2},{2,3},{3,4},{4,5},{5,6},{6,7},{7,0},{8,9},{9,10},{10,1... | collective-permute-start | bytes 3145736 | tf_op jit(solution)/shard_map/ppermute | solution.py:18
  51.5 7.7 %copy-start.4 = (bf16[1024,4,128]{2,1,0:T(4,128)(2,1)S(1)}, bf16[1024,4,128]{2,1,0:T(4,128)(2,1)}, u32[]{:S(2)}) copy-start(bf16[1024,4,128]{2,1,0:T(4,128)(2,1)} %param.5) | copy-start | bytes 3145732
  64.5 29.6 %all-to-all-start = ((f32[2,32,2048]{2,0,1:T(2,128)}), f32[2,32,2048]{2,0,1:T(2,128)}, u32[]{:S(2)}, u32[]{:S(2)}) async-start(f32[2,32,2048]{2,0,1:T(2,128)} %copy.84), calls=%async_computation | async-start | bytes 1048576 | tf_op jit(solution)/shard_map/all_to_all | solution.py:58
  76.7 1.0 copy-start.9
  78.6 4.0 %copy-start.5 = (bf16[1024,4,128]{2,1,0:T(4,128)(2,1)S(1)}, bf16[1024,4,128]{2,1,0:T(4,128)(2,1)}, u32[]{:S(2)}) copy-start(bf16[1024,4,128]{2,1,0:T(4,128)(2,1)} %param.7) | copy-start | bytes 3145732
  98.5 23.4 %all-to-all-start.1 = ((f32[2,32,2048]{2,0,1:T(2,128)}), f32[2,32,2048]{2,0,1:T(2,128)S(1)}, u32[]{:S(2)}, u32[]{:S(2)}) async-start(f32[2,32,2048]{2,0,1:T(2,128)} %copy.87), calls=%async_computation.1 | async-start | bytes 1048576 | tf_op jit(solution)/shard_map/all_to_all | solution.py:61
  103.9 4.1 %copy-start = (bf16[1024,4,128]{2,1,0:T(4,128)(2,1)S(1)}, bf16[1024,4,128]{2,1,0:T(4,128)(2,1)}, u32[]{:S(2)}) copy-start(bf16[1024,4,128]{2,1,0:T(4,128)(2,1)} %param.6) | copy-start | bytes 3145732
  103.9 4.1 %copy-start.1 = (bf16[4,4,256,256]{3,2,1,0:T(8,128)(2,1)S(1)}, bf16[4,4,256,256]{3,2,1,0:T(8,128)(2,1)}, u32[]{:S(2)}) copy-start(bf16[4,4,256,256]{3,2,1,0:T(8,128)(2,1)} %select_convert_fusion.1) | copy-start | bytes 6291460
  126.1 5.5 %copy-start.3 = (f32[4,4,256,128]{3,2,1,0:T(8,128)S(1)}, f32[4,4,256,128]{3,2,1,0:T(8,128)}, u32[]{:S(2)}) copy-start(f32[4,4,256,128]{3,2,1,0:T(8,128)} %fusion.27) | copy-start | bytes 6291460
  128.6 3.1 %copy-start.6 = (bf16[1024,4,128]{2,1,0:T(4,128)(2,1)S(1)}, bf16[1024,4,128]{2,1,0:T(4,128)(2,1)}, u32[]{:S(2)}) copy-start(bf16[1024,4,128]{2,1,0:T(4,128)(2,1)} %param.7) | copy-start | bytes 3145732
  132.2 1.9 %copy-start.2 = (f32[4,4,256,128]{3,2,1,0:T(8,128)S(1)}, f32[4,4,256,128]{3,2,1,0:T(8,128)}, u32[]{:S(2)}) copy-start(f32[4,4,256,128]{3,2,1,0:T(8,128)} %fusion.38) | copy-start | bytes 6291460
  132.2 1.9 %copy-start.7 = (bf16[4,256,4,128]{3,1,2,0:T(8,128)(2,1)S(1)}, bf16[4,256,4,128]{3,1,2,0:T(8,128)(2,1)}, u32[]{:S(2)}) copy-start(bf16[4,256,4,128]{3,1,2,0:T(8,128)(2,1)} %copy.76) | copy-start | bytes 3145732
  132.2 2.4 %slice-start = ((f32[4,4,128,128]{3,2,1,0:T(8,128)}), f32[3,4,128,128]{3,2,1,0:T(8,128)S(1)}, s32[]{:S(2)}) async-start(f32[4,4,128,128]{3,2,1,0:T(8,128)} %copy-done.9), calls=%async_computation.2 | async-start | bytes 1572864 | tf_op jit(solution)/shard_map/slice | solution.py:69
  132.2 2.5 %copy-start.10 = (f32[1,32,2048]{2,0,1:T(1,128)S(1)}, f32[1,32,2048]{2,0,1:T(1,128)}, u32[]{:S(2)}) copy-start(f32[1,32,2048]{2,0,1:T(1,128)} %get-tuple-element.13) | copy-start | bytes 786436
